TPU v7x, 32 devices: a whole 2x2x4 slice. The times are simulated.
32 devices in a mesh: dp: 16 (over z, y, x), fsdp: 2 (over core).
Axes of the slice: x: 2, y: 2, z: 4, core: 2. Of those that a mesh axis runs over, the one named last changes fastest.
Arguments:
- cells: bfloat16 [4096, 13500], P(('dp', 'fsdp')), may hold values from -6 to 6
- coordinates: float32 [2, 4096], P(None, ('dp', 'fsdp')), may hold values from 0 to 100
- slide_ids: int32 [32, 128], P(('dp', 'fsdp')), may hold values from 0 to 7, never falling along the last dimension, each value on 1 to 32 neighbouring positions
- live_mask: int32 [32, 128], P(('dp', 'fsdp')), may hold values from 0 to 1, as said below
- components: int32 [4096], P(('dp', 'fsdp')), may hold values from 0 to 15
- noise: float32 [4096, 512], P(('dp', 'fsdp')), may hold values from -6 to 6
- ramp_weight: float32 [], replicated, may hold values from 0.3 to 1
- embed_weight: bfloat16 [1024, 13500], P(('dp', 'fsdp')), may hold values from -0.0546875 to 0.0546875
- query_key_value: bfloat16 [1024, 3072], P(('dp', 'fsdp')), may hold values from -0.1875 to 0.1875
- output_weight: bfloat16 [1024, 1024], P(('dp', 'fsdp')), may hold values from -0.5 to 0.5
- up_weight: bfloat16 [1024, 4096], P(('dp', 'fsdp')), may hold values from -0.1875 to 0.1875
- up_bias: bfloat16 [4096], P(('dp', 'fsdp')), may hold values from -3 to 3
- down_weight: bfloat16 [4096, 1024], P(('dp', 'fsdp')), may hold values from -0.09375 to 0.09375
- down_bias: bfloat16 [1024], P(('dp', 'fsdp')), may hold values from -3 to 3
- first_gain: bfloat16 [1024], P(('dp', 'fsdp')), may hold values from 0.25 to 1.75
- first_shift: bfloat16 [1024], P(('dp', 'fsdp')), may hold values from -3 to 3
- second_gain: bfloat16 [1024], P(('dp', 'fsdp')), may hold values from 0.25 to 1.75
- second_shift: bfloat16 [1024], P(('dp', 'fsdp')), may hold values from -3 to 3
- encoder_weight: bfloat16 [1024, 1024], P(('dp', 'fsdp')), may hold values from -0.09375 to 0.09375
- encoder_bias: bfloat16 [1024], P(('dp', 'fsdp')), may hold values from -3 to 3
- prior_mean: bfloat16 [16, 512], P(None, ('dp', 'fsdp')), may hold values from -3 to 3
- prior_logvar: bfloat16 [16, 512], P(None, ('dp', 'fsdp')), may hold values from -1.5 to 1.5
- decoder_weight: bfloat16 [512, 13500], P(('dp', 'fsdp')), may hold values from -0.25 to 0.25
Outputs:
- loss: float32 [], replicated
- cells_grad: bfloat16 [4096, 13500], P(('dp', 'fsdp'))
- embed_weight_grad: float32 [1024, 13500], P(('dp', 'fsdp'))
- query_key_value_grad: float32 [1024, 3072], P(('dp', 'fsdp'))
- output_weight_grad: float32 [1024, 1024], P(('dp', 'fsdp'))
- up_weight_grad: float32 [1024, 4096], P(('dp', 'fsdp'))
- up_bias_grad: float32 [4096], P(('dp', 'fsdp'))
- down_weight_grad: float32 [4096, 1024], P(('dp', 'fsdp'))
- down_bias_grad: float32 [1024], P(('dp', 'fsdp'))
- first_gain_grad: float32 [1024], P(('dp', 'fsdp'))
- first_shift_grad: float32 [1024], P(('dp', 'fsdp'))
- second_gain_grad: float32 [1024], P(('dp', 'fsdp'))
- second_shift_grad: float32 [1024], P(('dp', 'fsdp'))
- encoder_weight_grad: float32 [1024, 1024], P(('dp', 'fsdp'))
- encoder_bias_grad: float32 [1024], P(('dp', 'fsdp'))
- prior_mean_grad: float32 [16, 512], P(None, ('dp', 'fsdp'))
- prior_logvar_grad: float32 [16, 512], P(None, ('dp', 'fsdp'))
- decoder_weight_grad: float32 [512, 13500], P(('dp', 'fsdp'))
Inputs may be any that keep to these rules, and one draw needn't show every extreme that they name: `live_mask`: in each row the live cells come first; the last row is all live.
All inputs are finite; a program needn't handle non-finite values.
Results may differ from a plain program's by a relative error of at most 0.025.
Values may be sent and summed in bfloat16 or wider, within the bound.
A program may use at most 384 MiB of HBM per device.

v0:
```python
import math
import jax
import jax.numpy as jnp
from jax import lax
from jax.sharding import PartitionSpec as P

D = 1024
HEAD_DIM = 64
GENES = 13500
LATENT = 512
NEG_SCORE = -1000000000.0
NORM_EPS = 1e-05
FREE_FLOOR = 1.0
FREE_TEMP = 0.25


def layer_norm(hidden, gain, shift):
    center = hidden - jnp.mean(hidden, axis=-1, keepdims=True)
    spread = jnp.mean(center * center, axis=-1, keepdims=True)
    return center * lax.rsqrt(spread + NORM_EPS) * gain + shift


def positions(coordinates):
    quarter = D // 4
    frequency = jnp.exp(jnp.arange(quarter, dtype=jnp.float32) * (-math.log(10000.0) / quarter))
    angle_x = coordinates[0][:, None] * frequency[None, :]
    angle_y = coordinates[1][:, None] * frequency[None, :]
    return jnp.concatenate(
        [jnp.sin(angle_x), jnp.cos(angle_x), jnp.sin(angle_y), jnp.cos(angle_y)], axis=1
    )


def matmul(left, right):
    return jnp.dot(left, right, preferred_element_type=jnp.float32)


def across(left, right):
    return lax.dot_general(
        left, right, (((1,), (1,)), ((), ())), preferred_element_type=jnp.float32
    )


def contract_rows(left, right):
    return lax.dot_general(
        left, right, (((0,), (0,)), ((), ())), preferred_element_type=jnp.float32
    )


def split_heads(joint):
    row_count = joint.shape[0]
    queries = joint[:, :D].reshape(row_count, -1, HEAD_DIM)
    keys = joint[:, D : 2 * D].reshape(row_count, -1, HEAD_DIM)
    values = joint[:, 2 * D :].reshape(row_count, -1, HEAD_DIM)
    return (queries, keys, values)


def masked_scores(queries, keys, allowed):
    scores = jnp.einsum(
        "qhd,khd->hqk", queries, keys, preferred_element_type=jnp.float32
    ) * HEAD_DIM ** (-0.5)
    return jnp.where(allowed[None], scores, NEG_SCORE)


def attention_forward(joint, allowed):
    queries, keys, values = split_heads(joint)
    masked = masked_scores(queries, keys, allowed)
    peak = jnp.max(masked, axis=-1, keepdims=True)
    raised = jnp.exp(masked - peak)
    denom = jnp.sum(raised, axis=-1, keepdims=True)
    probs = raised / denom
    logsum = peak + jnp.log(denom)
    context = jnp.einsum(
        "hqk,khd->qhd", probs.astype(jnp.bfloat16), values, preferred_element_type=jnp.float32
    )
    return (context.reshape(joint.shape[0], D).astype(jnp.bfloat16), logsum)


def attention_backward(joint, allowed, logsum, context_grad):
    row_count = joint.shape[0]
    queries, keys, values = split_heads(joint)
    probs = jnp.exp(masked_scores(queries, keys, allowed) - logsum)
    probs_low = probs.astype(jnp.bfloat16)
    incoming = context_grad.reshape(row_count, -1, HEAD_DIM)
    value_grad = jnp.einsum("hqk,qhd->khd", probs_low, incoming, preferred_element_type=jnp.float32)
    prob_grad = jnp.einsum("qhd,khd->hqk", incoming, values, preferred_element_type=jnp.float32)
    score_grad = (probs * (prob_grad - jnp.sum(probs * prob_grad, axis=-1, keepdims=True))).astype(
        jnp.bfloat16
    )
    query_grad = jnp.einsum(
        "hqk,khd->qhd", score_grad, keys, preferred_element_type=jnp.float32
    ) * HEAD_DIM ** (-0.5)
    key_grad = jnp.einsum(
        "hqk,qhd->khd", score_grad, queries, preferred_element_type=jnp.float32
    ) * HEAD_DIM ** (-0.5)
    return jnp.concatenate(
        [
            query_grad.reshape(row_count, D),
            key_grad.reshape(row_count, D),
            value_grad.reshape(row_count, D),
        ],
        axis=1,
    ).astype(jnp.bfloat16)


def shards(
    cells,
    coordinates,
    slide_ids,
    live_mask,
    components,
    noise,
    ramp_weight,
    embed_weight,
    query_key_value,
    output_weight,
    up_weight,
    up_bias,
    down_weight,
    down_bias,
    first_gain,
    first_shift,
    second_gain,
    second_shift,
    encoder_weight,
    encoder_bias,
    prior_mean,
    prior_logvar,
    decoder_weight,
):
    row_count = cells.shape[0]
    cell_total = row_count * lax.axis_size("dp") * lax.axis_size("fsdp")
    live = live_mask[0].astype(jnp.float32)
    slides = slide_ids[0]
    places = jnp.arange(row_count)
    allowed = (slides[:, None] == slides[None, :]) & (
        (live[None, :] > 0.5) | (places[:, None] == places[None, :])
    )
    onehot = (
        components[:, None] == jnp.arange(prior_mean.shape[0], dtype=jnp.int32)[None, :]
    ).astype(jnp.float32)
    middle = (
        lax.all_gather(query_key_value, ("dp", "fsdp"), axis=0, tiled=True),
        lax.all_gather(output_weight, ("dp", "fsdp"), axis=0, tiled=True),
        lax.all_gather(up_weight, ("dp", "fsdp"), axis=0, tiled=True),
        lax.all_gather(up_bias, ("dp", "fsdp"), axis=0, tiled=True),
        lax.all_gather(down_weight, ("dp", "fsdp"), axis=0, tiled=True),
        lax.all_gather(down_bias, ("dp", "fsdp"), axis=0, tiled=True),
        lax.all_gather(first_gain, ("dp", "fsdp"), axis=0, tiled=True),
        lax.all_gather(first_shift, ("dp", "fsdp"), axis=0, tiled=True),
        lax.all_gather(second_gain, ("dp", "fsdp"), axis=0, tiled=True),
        lax.all_gather(second_shift, ("dp", "fsdp"), axis=0, tiled=True),
        lax.all_gather(encoder_weight, ("dp", "fsdp"), axis=0, tiled=True),
        lax.all_gather(encoder_bias, ("dp", "fsdp"), axis=0, tiled=True),
        lax.all_gather(prior_mean, ("dp", "fsdp"), axis=1, tiled=True),
        lax.all_gather(prior_logvar, ("dp", "fsdp"), axis=1, tiled=True),
    )
    (
        joint_full,
        output_full,
        up_full,
        up_bias_full,
        down_full,
        down_bias_full,
        gain_first,
        shift_first,
        gain_second,
        shift_second,
        encoder_full,
        encoder_bias_full,
        prior_mean_full,
        prior_logvar_full,
    ) = middle
    gain_first = gain_first.astype(jnp.float32)
    shift_first = shift_first.astype(jnp.float32)
    gain_second = gain_second.astype(jnp.float32)
    shift_second = shift_second.astype(jnp.float32)
    cells_pair, embed_half, decoder_half = (
        lax.all_to_all(cells, "fsdp", split_axis=1, concat_axis=0, tiled=True),
        lax.all_to_all(embed_weight, "fsdp", split_axis=1, concat_axis=0, tiled=True),
        lax.all_to_all(decoder_weight, "fsdp", split_axis=1, concat_axis=0, tiled=True),
    )
    embed_cols, decoder_cols = (
        lax.all_gather(embed_half, "dp", axis=0, tiled=True),
        lax.all_gather(decoder_half, "dp", axis=0, tiled=True),
    )
    embedded = lax.psum_scatter(
        across(cells_pair, embed_cols), "fsdp", scatter_dimension=0, tiled=True
    )
    start_state = embedded + positions(coordinates)
    normed_first = layer_norm(start_state, gain_first, shift_first).astype(jnp.bfloat16)
    joint = matmul(normed_first, joint_full).astype(jnp.bfloat16)
    context, logsum = attention_forward(joint, allowed)
    middle_state = start_state + matmul(context, output_full)
    normed_second = layer_norm(middle_state, gain_second, shift_second).astype(jnp.bfloat16)
    pre = matmul(normed_second, up_full) + up_bias_full.astype(jnp.float32)
    active = jax.nn.gelu(pre, approximate=True).astype(jnp.bfloat16)
    end_state = middle_state + (matmul(active, down_full) + down_bias_full.astype(jnp.float32))
    end_low = end_state.astype(jnp.bfloat16)
    encoded = matmul(end_low, encoder_full) + encoder_bias_full.astype(jnp.float32)
    latent_mean = encoded[:, :LATENT]
    latent_logvar = encoded[:, LATENT:]
    latent = (latent_mean + jnp.exp(0.5 * latent_logvar) * noise).astype(jnp.bfloat16)
    latent_pair, live_rows = (
        lax.all_gather(latent, "fsdp", axis=0, tiled=True),
        lax.all_gather(live_mask, "fsdp", axis=0, tiled=True),
    )
    live_used = live_rows.reshape(-1).astype(jnp.float32)
    recon = matmul(latent_pair, decoder_cols)
    miss = recon - cells_pair.astype(jnp.float32)
    recon_local = jnp.sum(live_used * (0.5 * jnp.sum(miss * miss, axis=1)))
    center = jnp.dot(onehot, prior_mean_full.astype(jnp.float32), precision=lax.Precision.HIGHEST)
    scale = jnp.dot(onehot, prior_logvar_full.astype(jnp.float32), precision=lax.Precision.HIGHEST)
    gap = latent_mean - center
    inverse = jnp.exp(-scale)
    grown = jnp.exp(latent_logvar)
    diverge = 0.5 * (scale - latent_logvar + (grown + gap * gap) * inverse - 1.0)
    diverge_sum, recon_total, count = lax.psum(
        (jnp.sum(live[:, None] * diverge, axis=0), recon_local, jnp.sum(live)), ("dp", "fsdp")
    )
    kl_mean = diverge_sum / count
    shifted = (kl_mean - FREE_FLOOR) / FREE_TEMP
    free = FREE_FLOOR + FREE_TEMP * jax.nn.softplus(shifted)
    loss = (recon_total / count + ramp_weight * jnp.sum(free)) / GENES
    ratio = cell_total / count
    target_grad = ratio * live_used[:, None] * miss
    recon_grad = target_grad.astype(jnp.bfloat16)
    latent_grad = lax.psum_scatter(
        across(recon_grad, decoder_cols).astype(jnp.bfloat16),
        "fsdp",
        scatter_dimension=0,
        tiled=True,
    ).astype(jnp.float32)
    kl_scale = ratio * ramp_weight * jax.nn.sigmoid(shifted)[None, :] * live[:, None]
    pulled = kl_scale * gap * inverse
    mean_grad = latent_grad + pulled
    logvar_grad = latent_grad * 0.5 * jnp.exp(0.5 * latent_logvar) * noise + kl_scale * 0.5 * (
        grown * inverse - 1.0
    )
    encoded_grad = jnp.concatenate([mean_grad, logvar_grad], axis=1).astype(jnp.bfloat16)
    prior_mean_grad = jnp.dot(onehot.T, -pulled, precision=lax.Precision.HIGHEST)
    prior_logvar_grad = jnp.dot(
        onehot.T,
        kl_scale * 0.5 * (1.0 - (grown + gap * gap) * inverse),
        precision=lax.Precision.HIGHEST,
    )
    encoder_weight_grad = contract_rows(end_low, encoded_grad)
    encoder_bias_grad = jnp.sum(encoded_grad.astype(jnp.float32), axis=0)
    end_grad = across(encoded_grad, encoder_full)
    branch_grad = end_grad.astype(jnp.bfloat16)
    down_weight_grad = contract_rows(active, branch_grad)
    down_bias_grad = jnp.sum(branch_grad.astype(jnp.float32), axis=0)
    active_grad = across(branch_grad, down_full)
    gelu_value, gelu_back = jax.vjp(lambda value: jax.nn.gelu(value, approximate=True), pre)
    pre_grad = gelu_back(active_grad)[0].astype(jnp.bfloat16)
    up_weight_grad = contract_rows(normed_second, pre_grad)
    up_bias_grad = jnp.sum(pre_grad.astype(jnp.float32), axis=0)
    second_out_grad = across(pre_grad, up_full)
    norm_value, second_back = jax.vjp(layer_norm, middle_state, gain_second, shift_second)
    state_part, second_gain_grad, second_shift_grad = second_back(second_out_grad)
    middle_grad = end_grad + state_part
    attend_grad = middle_grad.astype(jnp.bfloat16)
    output_weight_grad = contract_rows(context, attend_grad)
    context_grad = across(attend_grad, output_full).astype(jnp.bfloat16)
    joint_grad = attention_backward(joint, allowed, logsum, context_grad)
    joint_weight_grad = contract_rows(normed_first, joint_grad)
    first_out_grad = across(joint_grad, joint_full)
    first_value, first_back = jax.vjp(layer_norm, start_state, gain_first, shift_first)
    start_part, first_gain_grad, first_shift_grad = first_back(first_out_grad)
    start_grad = middle_grad + start_part
    start_low = start_grad.astype(jnp.bfloat16)
    shared = (
        lax.psum_scatter(joint_weight_grad, ("dp", "fsdp"), scatter_dimension=0, tiled=True),
        lax.psum_scatter(output_weight_grad, ("dp", "fsdp"), scatter_dimension=0, tiled=True),
        lax.psum_scatter(up_weight_grad, ("dp", "fsdp"), scatter_dimension=0, tiled=True),
        lax.psum_scatter(up_bias_grad, ("dp", "fsdp"), scatter_dimension=0, tiled=True),
        lax.psum_scatter(down_weight_grad, ("dp", "fsdp"), scatter_dimension=0, tiled=True),
        lax.psum_scatter(down_bias_grad, ("dp", "fsdp"), scatter_dimension=0, tiled=True),
        lax.psum_scatter(first_gain_grad, ("dp", "fsdp"), scatter_dimension=0, tiled=True),
        lax.psum_scatter(first_shift_grad, ("dp", "fsdp"), scatter_dimension=0, tiled=True),
        lax.psum_scatter(second_gain_grad, ("dp", "fsdp"), scatter_dimension=0, tiled=True),
        lax.psum_scatter(second_shift_grad, ("dp", "fsdp"), scatter_dimension=0, tiled=True),
        lax.psum_scatter(encoder_weight_grad, ("dp", "fsdp"), scatter_dimension=0, tiled=True),
        lax.psum_scatter(encoder_bias_grad, ("dp", "fsdp"), scatter_dimension=0, tiled=True),
        lax.psum_scatter(prior_mean_grad, ("dp", "fsdp"), scatter_dimension=1, tiled=True),
        lax.psum_scatter(prior_logvar_grad, ("dp", "fsdp"), scatter_dimension=1, tiled=True),
    )
    start_pair = lax.all_gather(start_low, "fsdp", axis=0, tiled=True)
    embed_term = contract_rows(start_pair, cells_pair)
    decoder_term_half = contract_rows(latent_pair, recon_grad)
    embed_block, decoder_block = (
        lax.psum_scatter(embed_term, "dp", scatter_dimension=0, tiled=True),
        lax.psum_scatter(decoder_term_half, "dp", scatter_dimension=0, tiled=True),
    )
    cells_half = matmul(start_pair, embed_cols) - target_grad
    embed_grad, decoder_grad, cells_back = (
        lax.all_to_all(
            embed_block.astype(jnp.bfloat16), "fsdp", split_axis=0, concat_axis=1, tiled=True
        ).astype(embed_block.dtype),
        lax.all_to_all(
            decoder_block.astype(jnp.bfloat16), "fsdp", split_axis=0, concat_axis=1, tiled=True
        ).astype(decoder_block.dtype),
        lax.all_to_all(
            cells_half.astype(jnp.bfloat16), "fsdp", split_axis=0, concat_axis=1, tiled=True
        ).astype(cells_half.dtype),
    )
    cells_grad = cells_back.astype(jnp.bfloat16)
    return (
        loss,
        cells_grad,
        embed_grad,
        shared[0],
        shared[1],
        shared[2],
        shared[3],
        shared[4],
        shared[5],
        shared[6],
        shared[7],
        shared[8],
        shared[9],
        shared[10],
        shared[11],
        shared[12],
        shared[13],
        decoder_grad,
    )


def solution(mesh):
    in_specs = (
        P(("dp", "fsdp"), None),
        P(None, ("dp", "fsdp")),
        P(("dp", "fsdp"), None),
        P(("dp", "fsdp"), None),
        P(("dp", "fsdp")),
        P(("dp", "fsdp"), None),
        P(),
        P(("dp", "fsdp"), None),
        P(("dp", "fsdp"), None),
        P(("dp", "fsdp"), None),
        P(("dp", "fsdp"), None),
        P(("dp", "fsdp")),
        P(("dp", "fsdp"), None),
        P(("dp", "fsdp")),
        P(("dp", "fsdp")),
        P(("dp", "fsdp")),
        P(("dp", "fsdp")),
        P(("dp", "fsdp")),
        P(("dp", "fsdp"), None),
        P(("dp", "fsdp")),
        P(None, ("dp", "fsdp")),
        P(None, ("dp", "fsdp")),
        P(("dp", "fsdp"), None),
    )
    out_specs = (
        P(),
        P(("dp", "fsdp"), None),
        P(("dp", "fsdp"), None),
        P(("dp", "fsdp"), None),
        P(("dp", "fsdp"), None),
        P(("dp", "fsdp"), None),
        P(("dp", "fsdp")),
        P(("dp", "fsdp"), None),
        P(("dp", "fsdp")),
        P(("dp", "fsdp")),
        P(("dp", "fsdp")),
        P(("dp", "fsdp")),
        P(("dp", "fsdp")),
        P(("dp", "fsdp"), None),
        P(("dp", "fsdp")),
        P(None, ("dp", "fsdp")),
        P(None, ("dp", "fsdp")),
        P(("dp", "fsdp"), None),
    )
    return jax.shard_map(shards, mesh=mesh, in_specs=in_specs, out_specs=out_specs, check_vma=False)
```

profile of v0, /device:TPU:14, one launch (start us, length us, event | category | flops | bytes accessed | tf_op | source)
XLA Modules:
  0.0 2623.5 jit_solution(14391396643759751765)
XLA Ops:
  8.1 2.7 all_to_all.80
  10.8 5.2 all_to_all.102
  16.1 2.7 all_to_all.76
  18.8 6.5 all_to_all.103
  25.3 26.2 copy.109
  51.4 2.8 pad.9
  54.7 124.2 %all-gather.10.cloned.1.call-done = bf16[1024,6750]{1,0:T(8,128)(2,1)} async-done(((bf16[64,6750]{1,0:T(8,128)(2,1)}), bf16[1024,6750]{1,0:T(8,128)(2,1)}) %all-gather.10.cloned.1.call-update) | async-done | bytes 13824016 | tf_op jit(solution)/shard_map/all_gather | solution.py:183
  179.0 8.2 fusion.75
  191.2 4.8 all_to_all.104
  196.1 1.8 all-gather
  199.8 42.7 %all-reduce.15 = (bf16[1024]{0:T(1024)(128)(2,1)S(1)}, bf16[1024]{0:T(1024)(128)(2,1)S(1)}, bf16[1024]{0:T(1024)(128)(2,1)S(1)}, bf16[1024]{0:T(1024)(128)(2,1)S...) all-reduce(bf16[1024]{0:T(1024)(128)(2,1)S(1)} %dynamic-update-slic, ...), channel_id=1, replica_groups=mesh['dp'=16,'fsdp'=2] {'dp','fsdp'}, use_global_device_ids=true, to_apply=%add.1 | all-reduce | flops 6144 | bytes 24576
  242.5 28.6 %all-gather.1 = bf16[32,1,128]{2,1,0:T(2,128)(2,1)S(1)} all-gather(bf16[1,1,128]{2,1,0:T(2,128)(2,1)S(1)} %bitcast.142), channel_id=1, replica_groups=mesh['dp'=16,'fsdp'=2] {'dp','fsdp'}, dimensions={0}, use_global_device_ids=true | all-gather | bytes 8448 | tf_op jit(solution)/shard_map/all_gather | solution.py:145
  271.3 39.2 %all_gather.74 = bf16[16,512]{0,1:T(8,128)(2,1)S(1)} all-gather(bf16[16,16]{0,1:T(8,128)(2,1)S(1)} %copy.91), channel_id=1, replica_groups=mesh['dp'=16,'fsdp'=2] {'dp','fsdp'}, dimensions={1}, use_global_device_ids=true | all-gather | bytes 16896 | tf_op jit(solution)/shard_map/all_gather | solution.py:154
  310.6 40.0 %all_gather.73 = bf16[16,512]{0,1:T(8,128)(2,1)} all-gather(bf16[16,16]{0,1:T(8,128)(2,1)S(1)} %copy.90), channel_id=1, replica_groups=mesh['dp'=16,'fsdp'=2] {'dp','fsdp'}, dimensions={1}, use_global_device_ids=true | all-gather | bytes 16896 | tf_op jit(solution)/shard_map/all_gather | solution.py:155
  354.3 3.9 convolution_convert_fusion
  360.0 2.2 fusion.74
  362.4 36.6 %all-gather.16.cloned.1.call-done = bf16[1024,4096]{1,0:T(8,128)(2,1)} async-done(((bf16[32,4096]{1,0:T(8,128)(2,1)}), bf16[1024,4096]{1,0:T(8,128)(2,1)}) %all-gather.16.cloned.1.call-update) | async-done | bytes 8388624 | tf_op jit(solution)/shard_map/all_gather | solution.py:144
  399.1 6.1 convolution_add_fusion
  405.2 73.0 %all-gather.18.cloned.1.call-done = bf16[4096,1024]{1,0:T(8,128)(2,1)} async-done(((bf16[128,1024]{1,0:T(8,128)(2,1)}), bf16[4096,1024]{1,0:T(8,128)(2,1)}) %all-gather.18.cloned.1.call-update) | async-done | bytes 8388624 | tf_op jit(solution)/shard_map/all_gather | solution.py:146
  478.2 5.6 fusion.12
  483.8 52.2 %all-gather.20.cloned.1.call-done = bf16[1024,1024]{1,0:T(8,128)(2,1)} async-done(((bf16[32,1024]{1,0:T(8,128)(2,1)}), bf16[1024,1024]{1,0:T(8,128)(2,1)}) %all-gather.20.cloned.1.call-update) | async-done | bytes 2097168 | tf_op jit(solution)/shard_map/all_gather | solution.py:152
  536.1 2.1 convolution_add_fusion.1
  539.3 41.8 %all-reduce.14 = (f32[]{:T(128)}, f32[512]{0:T(512)}) all-reduce(f32[]{:T(128)} %convert_reduce_fusion.3, f32[512]{0:T(512)} %get-tuple-element.51), channel_id=1, replica_groups=mesh['dp'=16,'fsdp'=2] {'dp','fsdp'}, use_global_device_ids=true, to_apply=%region_11.12 | all-reduce | flops 513 | bytes 4104 | tf_op jit(solution)/shard_map/psum | solution.py:217
  581.8 2.5 all_gather.71
  584.3 54.2 %all-gather.22.cloned.1.call-done = bf16[512,6750]{1,0:T(8,128)(2,1)} async-done(((bf16[32,6750]{1,0:T(8,128)(2,1)}), bf16[512,6750]{1,0:T(8,128)(2,1)}) %all-gather.22.cloned.1.call-update) | async-done | bytes 6912016 | tf_op jit(solution)/shard_map/all_gather | solution.py:184
  638.5 7.5 multiply_reduce_fusion
  646.6 2.2 copy-done
  648.8 2.8 fusion.15
  656.1 10.2 fusion.9
  667.6 1.4 fusion.24
  669.7 2.6 fusion.41
  672.3 7.8 convert_reduce_fusion
  680.2 3.5 multiply_reduce_fusion.2
  685.3 1.5 convolution_convert_fusion.2
  686.9 1.8 copy.92
  688.7 1.4 multiply_reduce_fusion.1
  691.9 5.8 multiply_reduce_fusion.3
  698.1 2.5 all_gather.75
  700.6 11.3 fusion.76
  712.9 2.6 fusion.34
  716.5 2.7 fusion.40
  720.4 6.5 fusion.22
  728.1 8.2 fusion.68
  736.4 1.5 copy-done.4
  737.9 8.2 fusion.59
  746.9 16.8 reduce-scatter.34.cloned.1.call-done
  765.0 130.2 %reduce-scatter.36.cloned.1.call-done = f32[16,16]{1,0:T(8,128)} async-done(((f32[512,16]{1,0:T(8,128)}), f32[16,16]{1,0:T(8,128)}) %reduce-scatter.36.cloned.1.call-update) | async-done | bytes 1040
  896.7 94.9 %all-reduce.13 = (f32[]{:T(128)}, f32[4096]{0:T(1024)S(1)}, f32[1024]{0:T(1024)S(1)}, f32[1024]{0:T(1024)S(1)}, f32[1024]{0:T(1024)S(1)}, /*index=5*/f32[1024]{0:T(1024)S(1)}, f32[1024]{0:T(1024)S(1)}, f32[1024]{0:T(1024)S(1)}) all-reduce(f32[]{:T(128)} %get-tuple-element.62, ...), channel_id=1, replica_groups=mesh['dp'=16,'fsdp'=2] {'dp','fsdp'}, use_global_device_ids=true, to_apply=%region_9.10 | all-reduce | flops 10241 | bytes 81928 | tf_op jit(solution)/shard_map/psum | solution.py:217
  993.0 14.4 fusion
  1007.4 6.4 all_to_all.88
  1014.3 6.5 all_to_all.105
  1020.8 2.4 all_to_all.91
  1027.3 190.2 %reduce-scatter.32.cloned.1.call-done = f32[32,6750]{1,0:T(8,128)} async-done(((f32[512,6750]{1,0:T(8,128)}), f32[32,6750]{1,0:T(8,128)}) %reduce-scatter.32.cloned.1.call-update) | async-done | bytes 864016 | tf_op jit(solution)/shard_map/reduce_scatter | solution.py:292
  1218.7 4.1 all_to_all.106
  1223.3 1.5 reshape.264
  1224.9 568.1 %reduce-scatter.20.cloned.1.call-done = f32[64,6750]{1,0:T(8,128)} async-done(((f32[1024,6750]{1,0:T(8,128)}), f32[64,6750]{1,0:T(8,128)}) %reduce-scatter.20.cloned.1.call-update) | async-done | bytes 1728016 | tf_op jit(solution)/shard_map/reduce_scatter | solution.py:291
  1793.0 1.6 convert_element_type.179
  1794.6 4.7 all_to_all.107
  1800.7 2.5 reshape.263
  1803.2 106.0 %reduce-scatter.24.cloned.1.call-done = f32[32,1024]{1,0:T(8,128)} async-done(((f32[1024,1024]{1,0:T(8,128)}), f32[32,1024]{1,0:T(8,128)}) %reduce-scatter.24.cloned.1.call-update) | async-done | bytes 131088 | tf_op jit(solution)/shard_map/reduce_scatter | solution.py:273
  1909.2 139.9 %reduce-scatter.30.cloned.1.call-done = f32[32,1024]{1,0:T(8,128)} async-done(((f32[1024,1024]{1,0:T(8,128)}), f32[32,1024]{1,0:T(8,128)}) %reduce-scatter.30.cloned.1.call-update) | async-done | bytes 131088 | tf_op jit(solution)/shard_map/reduce_scatter | solution.py:282
  2049.1 190.8 %reduce-scatter.22.cloned.1.call-done = f32[32,3072]{1,0:T(8,128)} async-done(((f32[1024,3072]{1,0:T(8,128)}), f32[32,3072]{1,0:T(8,128)}) %reduce-scatter.22.cloned.1.call-update) | async-done | bytes 393232 | tf_op jit(solution)/shard_map/reduce_scatter | solution.py:272
  2239.9 187.3 %reduce-scatter.26.cloned.1.call-done = f32[32,4096]{1,0:T(8,128)} async-done(((f32[1024,4096]{1,0:T(8,128)}), f32[32,4096]{1,0:T(8,128)}) %reduce-scatter.26.cloned.1.call-update) | async-done | bytes 524304 | tf_op jit(solution)/shard_map/reduce_scatter | solution.py:274
  2427.2 187.3 %reduce-scatter.28.cloned.1.call-done = f32[128,1024]{1,0:T(8,128)} async-done(((f32[4096,1024]{1,0:T(8,128)}), f32[128,1024]{1,0:T(8,128)}) %reduce-scatter.28.cloned.1.call-update) | async-done | bytes 524304 | tf_op jit(solution)/shard_map/reduce_scatter | solution.py:276
  (286 shorter events, 38.4 us)
Async XLA Ops:
  8.0 170.9 %all-gather.10.cloned.1.call-start = ((), (), s32[]{:S(2)}) async-start(), calls=%async_computation.17 | async-start | bytes 14761984 | tf_op jit(solution)/shard_map/all_gather | solution.py:183
  16.1 336.7 %reduce-scatter.16.cloned.1.call-start = ((), (), s32[]{:S(2)}) async-start(), calls=%async_computation.18 | async-start | bytes 1572864 | tf_op jit(solution)/shard_map/reduce_scatter | solution.py:186
  54.7 132.5 %copy-start.1 = (bf16[844,8,2,128]{3,1,2,0:T(8,128)(2,1)}, bf16[844,8,2,128]{3,1,2,0:T(8,128)(2,1)S(1)}, u32[]{:S(2)}) copy-start(bf16[844,8,2,128]{3,1,2,0:T(8,128)(2,1)S(1)} %copy.107) | copy-start | bytes 10371076
  187.2 8.9 copy-start.78
  187.2 11.2 copy-start.72
  187.3 11.4 copy-start.73
  187.3 11.6 copy-start.74
  187.3 11.8 copy-start.75
  187.3 12.1 copy-start.76
  187.3 12.3 copy-start.77
  187.3 55.2 %copy-start.67 = (bf16[128]{0:T(256)(128)(2,1)S(1)}, bf16[128]{0:T(256)(128)(2,1)}, u32[]{:S(2)}) copy-start(bf16[128]{0:T(256)(128)(2,1)} %param.34) | copy-start | bytes 772
  187.3 83.8 %copy-start.58 = (bf16[16,16]{1,0:T(8,128)(2,1)S(1)}, bf16[16,16]{1,0:T(8,128)(2,1)}, u32[]{:S(2)}) copy-start(bf16[16,16]{1,0:T(8,128)(2,1)} %param.43) | copy-start | bytes 1540
  187.3 83.9 %copy-start.59 = (bf16[16,16]{1,0:T(8,128)(2,1)S(1)}, bf16[16,16]{1,0:T(8,128)(2,1)}, u32[]{:S(2)}) copy-start(bf16[16,16]{1,0:T(8,128)(2,1)} %param.44) | copy-start | bytes 1540
  187.3 166.9 %all-gather.12.cloned.1.call-start = ((), (), s32[]{:S(2)}) async-start(), calls=%async_computation.19 | async-start | bytes 6488064 | tf_op jit(solution)/shard_map/all_gather | solution.py:142
  187.9 163.7 %copy-start.65 = (f32[2,128]{1,0:T(2,128)S(1)}, f32[2,128]{1,0:T(2,128)}, u32[]{:S(2)}) copy-start(f32[2,128]{1,0:T(2,128)} %param.24) | copy-start | bytes 3076
  187.9 163.7 %copy-start.63 = (s32[1,128]{1,0:T(1,128)S(1)}, s32[1,128]{1,0:T(1,128)}, u32[]{:S(2)}) copy-start(s32[1,128]{1,0:T(1,128)} %param.25) | copy-start | bytes 1540
  188.0 172.0 %all-gather.14.cloned.1.call-start = ((), (), s32[]{:S(2)}) async-start(), calls=%async_computation.20 | async-start | bytes 2162688 | tf_op jit(solution)/shard_map/all_gather | solution.py:143
  188.5 210.5 %all-gather.16.cloned.1.call-start = ((), (), s32[]{:S(2)}) async-start(), calls=%async_computation.21 | async-start | bytes 8650752 | tf_op jit(solution)/shard_map/all_gather | solution.py:144
  189.1 289.1 %all-gather.18.cloned.1.call-start = ((), (), s32[]{:S(2)}) async-start(), calls=%async_computation.22 | async-start | bytes 8650752 | tf_op jit(solution)/shard_map/all_gather | solution.py:146
  189.9 346.2 %all-gather.20.cloned.1.call-start = ((), (), s32[]{:S(2)}) async-start(), calls=%async_computation.23 | async-start | bytes 2162688 | tf_op jit(solution)/shard_map/all_gather | solution.py:152
  190.6 447.9 %all-gather.22.cloned.1.call-start = ((), (), s32[]{:S(2)}) async-start(), calls=%async_computation.24 | async-start | bytes 7380992 | tf_op jit(solution)/shard_map/all_gather | solution.py:184
  196.0 471.6 %reduce-scatter.18.cloned.1.call-start = ((), (), s32[]{:S(2)}) async-start(), calls=%async_computation.25 | async-start | bytes 393216 | tf_op jit(solution)/shard_map/reduce_scatter | solution.py:227
  354.0 4.2 copy-start.46
  354.2 4.0 copy-start.68
  354.2 3.9 copy-start.54
  360.0 45.2 %copy-start.16 = (bf16[16,64,128]{2,1,0:T(8,128)(2,1)}, bf16[16,64,128]{2,1,0:T(8,128)(2,1)S(1)}, u32[]{:S(2)}) copy-start(bf16[16,64,128]{2,1,0:T(8,128)(2,1)S(1)} %convolution_convert_fusion.3) | copy-start | bytes 786436
  362.2 43.0 %copy-start.36 = (f32[128]{0:T(128)}, f32[128]{0:T(128)S(1)}, u32[]{:S(2)}) copy-start(f32[128]{0:T(128)S(1)} %broadcast_multiply_fusion.1) | copy-start | bytes 1540
  362.4 42.8 %copy-start.70 = (f32[128]{0:T(128)}, f32[128]{0:T(128)S(1)}, u32[]{:S(2)}) copy-start(f32[128]{0:T(128)S(1)} %multiply_reduce_fusion.6) | copy-start | bytes 1540
  362.4 42.7 %copy-start.39 = (f32[128]{0:T(128)}, f32[128]{0:T(128)S(1)}, u32[]{:S(2)}) copy-start(f32[128]{0:T(128)S(1)} %fusion.54) | copy-start | bytes 1540
  483.8 52.2 %copy-start.26 = (bf16[128,1024]{1,0:T(8,128)(2,1)}, bf16[128,1024]{1,0:T(8,128)(2,1)S(1)}, u32[]{:S(2)}) copy-start(bf16[128,1024]{1,0:T(8,128)(2,1)S(1)} %fusion.12) | copy-start | bytes 786436
  483.8 54.3 %copy-start.51 = (s32[128]{0:T(128)S(1)}, s32[128]{0:T(128)}, u32[]{:S(2)}) copy-start(s32[128]{0:T(128)} %param.27) | copy-start | bytes 1540
  584.3 61.6 %copy-start.60 = (f32[2,1,128]{2,1,0:T(1,128)S(1)}, f32[2,1,128]{2,1,0:T(1,128)}, u32[]{:S(2)}) copy-start(f32[2,1,128]{2,1,0:T(1,128)} %convert_element_type.194) | copy-start | bytes 3076
  638.5 10.4 copy-start.6
  646.6 9.5 copy-start.49
  648.8 4.8 copy-start.53
  651.6 112.1 %reduce-scatter.34.cloned.1.call-start = ((), (), s32[]{:S(2)}) async-start(), calls=%async_computation.33 | async-start | bytes 270336
  651.7 14.6 copy-start.57
  653.6 12.7 copy-start.33
  654.8 240.4 %reduce-scatter.36.cloned.1.call-start = ((), (), s32[]{:S(2)}) async-start(), calls=%async_computation.34 | async-start | bytes 270336
  656.1 561.4 %reduce-scatter.32.cloned.1.call-start = ((), (), s32[]{:S(2)}) async-start(), calls=%async_computation.32 | async-start | bytes 14761984 | tf_op jit(solution)/shard_map/reduce_scatter | solution.py:292
  666.4 1126.6 %reduce-scatter.20.cloned.1.call-start = ((), (), s32[]{:S(2)}) async-start(), calls=%async_computation.26 | async-start | bytes 29523968 | tf_op jit(solution)/shard_map/reduce_scatter | solution.py:291
  667.6 4.6 copy-start.3
  669.7 10.4 slice-start
  672.3 7.8 slice-start.1
  672.3 7.8 copy-start.37
  672.3 7.8 copy-start.40
  691.0 6.6 copy-start.19
  691.3 6.3 copy-start.21
  691.8 5.8 copy-start.23
  691.9 5.8 copy-start.69
  700.6 11.3 copy-start.9
  712.0 1197.2 %reduce-scatter.24.cloned.1.call-start = ((), (), s32[]{:S(2)}) async-start(), calls=%async_computation.28 | async-start | bytes 4325376 | tf_op jit(solution)/shard_map/reduce_scatter | solution.py:273
  715.6 1333.5 %reduce-scatter.30.cloned.1.call-start = ((), (), s32[]{:S(2)}) async-start(), calls=%async_computation.31 | async-start | bytes 4325376 | tf_op jit(solution)/shard_map/reduce_scatter | solution.py:282
  719.3 1520.6 %reduce-scatter.22.cloned.1.call-start = ((), (), s32[]{:S(2)}) async-start(), calls=%async_computation.27 | async-start | bytes 12976128 | tf_op jit(solution)/shard_map/reduce_scatter | solution.py:272
  726.9 1700.3 %reduce-scatter.26.cloned.1.call-start = ((), (), s32[]{:S(2)}) async-start(), calls=%async_computation.29 | async-start | bytes 17301504 | tf_op jit(solution)/shard_map/reduce_scatter | solution.py:274
  736.4 1878.1 %reduce-scatter.28.cloned.1.call-start = ((), (), s32[]{:S(2)}) async-start(), calls=%async_computation.30 | async-start | bytes 17301504 | tf_op jit(solution)/shard_map/reduce_scatter | solution.py:276
  746.1 150.5 %copy-start.42 = (f32[1024]{0:T(1024)S(1)}, f32[1024]{0:T(1024)}, u32[]{:S(2)}) copy-start(f32[1024]{0:T(1024)} %get-tuple-element.18) | copy-start | bytes 12292
  746.1 150.6 %copy-start.43 = (f32[1024]{0:T(1024)S(1)}, f32[1024]{0:T(1024)}, u32[]{:S(2)}) copy-start(f32[1024]{0:T(1024)} %get-tuple-element.22) | copy-start | bytes 12292
  746.1 150.6 %copy-start.44 = (f32[1024]{0:T(1024)S(1)}, f32[1024]{0:T(1024)}, u32[]{:S(2)}) copy-start(f32[1024]{0:T(1024)} %get-tuple-element.50) | copy-start | bytes 12292
  746.1 150.6 %copy-start.45 = (f32[4096]{0:T(1024)S(1)}, f32[4096]{0:T(1024)}, u32[]{:S(2)}) copy-start(f32[4096]{0:T(1024)} %get-tuple-element.74) | copy-start | bytes 49156
  746.1 150.6 %copy-start.61 = (f32[1024]{0:T(1024)S(1)}, f32[1024]{0:T(1024)}, u32[]{:S(2)}) copy-start(f32[1024]{0:T(1024)} %get-tuple-element.20) | copy-start | bytes 12292
  746.1 150.6 %copy-start.62 = (f32[1024]{0:T(1024)S(1)}, f32[1024]{0:T(1024)}, u32[]{:S(2)}) copy-start(f32[1024]{0:T(1024)} %get-tuple-element.23) | copy-start | bytes 12292
  746.1 246.8 %copy-start.10 = (bf16[256,1024]{1,0:T(8,128)(2,1)S(1)}, bf16[256,1024]{1,0:T(8,128)(2,1)}, u32[]{:S(2)}) copy-start(bf16[256,1024]{1,0:T(8,128)(2,1)} %copy-done.9) | copy-start | bytes 1572868
  746.1 246.8 %copy-start.50 = (f32[256]{0:T(256)S(1)}, f32[256]{0:T(256)}, u32[]{:S(2)}) copy-start(f32[256]{0:T(256)} %copy-done.49) | copy-start | bytes 3076
  (36 other events, 59.4 us)
Sparse Core Ops, SparseCore 0:
  16.2 162.7 all-gather.9
  187.3 9.7 reduce-scatter.15
  651.7 7.7 reduce-scatter.17
  661.6 102.0 reduce-scatter.33
  765.8 129.3 reduce-scatter.35
  897.4 320.1 reduce-scatter.31
  1219.9 573.0 reduce-scatter.19
  1795.9 113.2 reduce-scatter.23
  1912.2 136.8 reduce-scatter.29
  2056.6 183.2 reduce-scatter.21
  2242.8 184.3 reduce-scatter.25
  2429.9 184.4 reduce-scatter.27
Sparse Core Ops, SparseCore 1:
  191.1 69.7 all-gather.11
  264.0 54.8 all-gather.13
  322.0 77.0 all-gather.15
  402.4 75.8 all-gather.17
  481.5 54.5 all-gather.19
  539.1 99.3 all-gather.21
where the time goes:
time: 2630 us; the launch traced here: 2620 us
  waiting for transfers between devices  2060 us (78%)
  blocking collectives  326 us (12%)
  matrix products  130 us (5%)
  local copies, waits for them, and re-layouts  71.3 us (3%)
    reduce_scatter x1, waiting for transfers between devices, shards(): lax.psum_scatter(embed_term, 'dp', scatter_dimension=0, tiled=True)  568 us
    reduce_scatter x1, waiting for transfers between devices, shards(): lax.psum_scatter(joint_weight_grad, ('dp', 'fsdp'), scatter_dimension=0,...  191 us
    reduce_scatter x1, waiting for transfers between devices, shards(): lax.psum_scatter(decoder_term_half, 'dp', scatter_dimension=0, tiled=True)  190 us
    reduce_scatter x1, waiting for transfers between devices, shards(): lax.psum_scatter(up_weight_grad, ('dp', 'fsdp'), scatter_dimension=0, til...  187 us
    reduce_scatter x1, waiting for transfers between devices, shards(): lax.psum_scatter(down_weight_grad, ('dp', 'fsdp'), scatter_dimension=0, t...  187 us
    unnamed x20, waiting for transfers between devices  150 us
    reduce_scatter x1, waiting for transfers between devices, shards(): lax.psum_scatter(encoder_weight_grad, ('dp', 'fsdp'), scatter_dimension=0...  140 us
    psum x2, blocking collectives, shards(): lax.psum((jnp.sum(live[:, None] * diverge, axis=0), recon_local, jnp.sum(...  137 us
  transfers between devices with their start and end apart: 18, of which 14 were waited for; matrix products, arithmetic and copies ran while one was open for 7% of the time, Pallas kernels for 0%

commit v1 on v0

--- a/solution.py
+++ b/solution.py
@@ -12,6 +12,24 @@
 NORM_EPS = 1e-05
 FREE_FLOOR = 1.0
 FREE_TEMP = 0.25
+
+
+def gather_around(value, axis, dim):
+    ways, here, step = (lax.axis_size(axis), lax.axis_index(axis), value.shape[dim])
+    shape = [n * ways if d == dim else n for d, n in enumerate(value.shape)]
+    full = lax.dynamic_update_slice_in_dim(
+        jnp.zeros(shape, value.dtype), value, here * step, axis=dim
+    )
+    going_up = going_down = value
+    for far in range(1, ways // 2 + 1):
+        going_up = lax.ppermute(going_up, axis, [(d, (d + 1) % ways) for d in range(ways)])
+        full = lax.dynamic_update_slice_in_dim(full, going_up, (here - far) % ways * step, axis=dim)
+        if 2 * far < ways:
+            going_down = lax.ppermute(going_down, axis, [(d, (d - 1) % ways) for d in range(ways)])
+            full = lax.dynamic_update_slice_in_dim(
+                full, going_down, (here + far) % ways * step, axis=dim
+            )
+    return full
 
 
 def layer_norm(hidden, gain, shift):
@@ -180,7 +198,7 @@
         lax.all_to_all(decoder_weight, "fsdp", split_axis=1, concat_axis=0, tiled=True),
     )
     embed_cols, decoder_cols = (
-        lax.all_gather(embed_half, "dp", axis=0, tiled=True),
+        gather_around(embed_half, "dp", 0),
         lax.all_gather(decoder_half, "dp", axis=0, tiled=True),
     )
     embedded = lax.psum_scatter(

time: 2630 us -> 2790 us (1.061)
  starting transfers between devices: 0.92 us -> 136 us
  waiting for transfers between devices: 2060 us -> 2030 us
  local copies, waits for them, and re-layouts: 71.3 us -> 99.9 us
    ppermute x0 -> x15, starting transfers between devices: none -> 131 us  [the longest x8 129 us: gather_around(): lax.ppermute(going_up, axis, [(d, (d + 1) % ways) for d in range(ways)])]
    all_gather x1 -> x0, waiting for transfers between devices: 124 us -> none  [shards(): lax.all_gather(embed_half, 'dp', axis=0, tiled=True)]
    ppermute x0 -> x15, waiting for transfers between devices: none -> 104 us  [the longest x8 104 us: gather_around(): lax.ppermute(going_up, axis, [(d, (d + 1) % ways) for d in range(ways)])]
    unnamed x20 -> x19, waiting for transfers between devices: 150 us -> 137 us
  transfers between devices with their start and end apart: 18 -> 33, of which waited for: 14 -> 21; matrix products, arithmetic and copies ran while one was open for 7% -> 8% of each run, Pallas kernels for 0% -> 0%
where the time goes in v1:
time: 2790 us; the launch traced here: 2780 us
  waiting for transfers between devices  2030 us (73%)
  blocking collectives  335 us (12%)
  matrix products  138 us (5%)
  starting transfers between devices  136 us (5%)
  local copies, waits for them, and re-layouts  99.9 us (4%)
    reduce_scatter x1, waiting for transfers between devices, shards(): lax.psum_scatter(embed_term, 'dp', scatter_dimension=0, tiled=True)  568 us
    reduce_scatter x1, waiting for transfers between devices, shards(): lax.psum_scatter(decoder_term_half, 'dp', scatter_dimension=0, tiled=True)  192 us
    reduce_scatter x1, waiting for transfers between devices, shards(): lax.psum_scatter(joint_weight_grad, ('dp', 'fsdp'), scatter_dimension=0,...  191 us
    reduce_scatter x1, waiting for transfers between devices, shards(): lax.psum_scatter(down_weight_grad, ('dp', 'fsdp'), scatter_dimension=0, t...  187 us
    reduce_scatter x1, waiting for transfers between devices, shards(): lax.psum_scatter(up_weight_grad, ('dp', 'fsdp'), scatter_dimension=0, til...  187 us
    reduce_scatter x1, waiting for transfers between devices, shards(): lax.psum_scatter(encoder_weight_grad, ('dp', 'fsdp'), scatter_dimension=0...  140 us
    unnamed x19, waiting for transfers between devices  137 us
    psum x2, blocking collectives, shards(): lax.psum((jnp.sum(live[:, None] * diverge, axis=0), recon_local, jnp.sum(...  135 us
  transfers between devices with their start and end apart: 33, of which 21 were waited for; matrix products, arithmetic and copies ran while one was open for 8% of the time, Pallas kernels for 0%

profile of v1, /device:TPU:14, one launch (start us, length us, event | category | flops | bytes accessed | tf_op | source)
XLA Modules:
  0.0 2784.5 jit_solution(1764792521630009736)
XLA Ops:
  8.0 2.7 all_to_all.76
  10.8 5.2 all_to_all.102
  18.0 4.4 all_to_all.80
  22.5 4.0 all-to-all-start.1
  26.8 3.5 all-to-all-done.1
  30.3 26.2 copy.139
  56.4 2.8 pad.9
  59.8 6.0 broadcast_in_dim.26
  68.0 3.3 collective-permute-start.2
  75.6 14.9 collective-permute-done.2
  90.5 18.8 collective-permute-start.4
  113.3 14.4 collective-permute-done.4
  127.7 20.9 collective-permute-start.6
  150.7 15.4 collective-permute-done.6
  166.2 21.0 collective-permute-start.8
  189.2 14.7 collective-permute-done.8
  203.9 21.0 collective-permute-start.10
  226.9 14.8 collective-permute-done.10
  241.7 21.0 collective-permute-start.12
  264.7 15.0 collective-permute-done.12
  279.6 21.0 collective-permute-start.14
  302.6 15.1 collective-permute-done.14
  318.7 8.1 convolution_bitcast_fusion
  331.8 4.8 all_to_all.103
  340.6 61.9 %all-reduce.15 = (bf16[1024]{0:T(1024)(128)(2,1)S(1)}, bf16[1024]{0:T(1024)(128)(2,1)S(1)}, bf16[1024]{0:T(1024)(128)(2,1)S(1)}, bf16[1024]{0:T(1024)(128)(2,1)S...) all-reduce(bf16[1024]{0:T(1024)(128)(2,1)S(1)} %dynamic-update-slic, ...), channel_id=1, replica_groups=mesh['dp'=16,'fsdp'=2] {'dp','fsdp'}, use_global_device_ids=true, to_apply=%add.1 | all-reduce | flops 6144 | bytes 24576
  402.6 28.7 %all-gather.1 = bf16[32,1,128]{2,1,0:T(2,128)(2,1)S(1)} all-gather(bf16[1,1,128]{2,1,0:T(2,128)(2,1)S(1)} %bitcast.143), channel_id=1, replica_groups=mesh['dp'=16,'fsdp'=2] {'dp','fsdp'}, dimensions={0}, use_global_device_ids=true | all-gather | bytes 8448 | tf_op jit(solution)/shard_map/all_gather | solution.py:163
  431.5 37.6 %all_gather.70 = bf16[16,512]{0,1:T(8,128)(2,1)S(1)} all-gather(bf16[16,16]{0,1:T(8,128)(2,1)S(1)} %copy.114), channel_id=1, replica_groups=mesh['dp'=16,'fsdp'=2] {'dp','fsdp'}, dimensions={1}, use_global_device_ids=true | all-gather | bytes 16896 | tf_op jit(solution)/shard_map/all_gather | solution.py:172
  469.1 39.7 %all_gather.69 = bf16[16,512]{0,1:T(8,128)(2,1)} all-gather(bf16[16,16]{0,1:T(8,128)(2,1)S(1)} %copy.113), channel_id=1, replica_groups=mesh['dp'=16,'fsdp'=2] {'dp','fsdp'}, dimensions={1}, use_global_device_ids=true | all-gather | bytes 16896 | tf_op jit(solution)/shard_map/all_gather | solution.py:173
  512.5 3.9 convolution_convert_fusion
  520.9 38.9 %all-gather.13.cloned.1.call-done = bf16[1024,4096]{1,0:T(8,128)(2,1)} async-done(((bf16[32,4096]{1,0:T(8,128)(2,1)}), bf16[1024,4096]{1,0:T(8,128)(2,1)}) %all-gather.13.cloned.1.call-update) | async-done | bytes 8388624 | tf_op jit(solution)/shard_map/all_gather | solution.py:162
  559.7 6.2 convolution_add_fusion
  565.9 73.0 %all-gather.15.cloned.1.call-done = bf16[4096,1024]{1,0:T(8,128)(2,1)} async-done(((bf16[128,1024]{1,0:T(8,128)(2,1)}), bf16[4096,1024]{1,0:T(8,128)(2,1)}) %all-gather.15.cloned.1.call-update) | async-done | bytes 8388624 | tf_op jit(solution)/shard_map/all_gather | solution.py:164
  638.9 7.2 fusion.12
  646.1 50.6 %all-gather.17.cloned.1.call-done = bf16[1024,1024]{1,0:T(8,128)(2,1)} async-done(((bf16[32,1024]{1,0:T(8,128)(2,1)}), bf16[1024,1024]{1,0:T(8,128)(2,1)}) %all-gather.17.cloned.1.call-update) | async-done | bytes 2097168 | tf_op jit(solution)/shard_map/all_gather | solution.py:170
  700.0 41.8 %all-reduce.14 = (f32[]{:T(128)}, f32[512]{0:T(512)}) all-reduce(f32[]{:T(128)} %convert_reduce_fusion.3, f32[512]{0:T(512)} %get-tuple-element.45), channel_id=1, replica_groups=mesh['dp'=16,'fsdp'=2] {'dp','fsdp'}, use_global_device_ids=true, to_apply=%region_11.12 | all-reduce | flops 513 | bytes 4104 | tf_op jit(solution)/shard_map/psum | solution.py:235
  744.9 54.2 %all-gather.19.cloned.1.call-done = bf16[512,6750]{1,0:T(8,128)(2,1)} async-done(((bf16[32,6750]{1,0:T(8,128)(2,1)}), bf16[512,6750]{1,0:T(8,128)(2,1)}) %all-gather.19.cloned.1.call-update) | async-done | bytes 6912016 | tf_op jit(solution)/shard_map/all_gather | solution.py:202
  799.1 7.4 multiply_reduce_fusion
  809.4 2.8 fusion.15
  816.7 10.0 fusion.9
  829.3 3.1 convert_reduce_fusion.2
  832.6 8.3 convert_reduce_fusion
  840.9 8.1 fusion.74
  862.3 6.5 fusion.73
  876.9 11.3 fusion.75
  889.1 2.6 fusion.76
  891.9 2.7 fusion.38
  894.7 6.4 fusion.22
  902.3 8.2 fusion.67
  912.1 8.2 fusion.57
  921.0 3.4 reduce-scatter.34.cloned.1.call-done
  925.8 130.3 %reduce-scatter.36.cloned.1.call-done = f32[16,16]{1,0:T(8,128)} async-done(((f32[512,16]{1,0:T(8,128)}), f32[16,16]{1,0:T(8,128)}) %reduce-scatter.36.cloned.1.call-update) | async-done | bytes 1040
  1057.5 93.2 %all-reduce.13 = (f32[]{:T(128)}, f32[4096]{0:T(1024)S(1)}, f32[1024]{0:T(1024)S(1)}, f32[1024]{0:T(1024)S(1)}, f32[1024]{0:T(1024)S(1)}, /*index=5*/f32[1024]{0:T(1024)S(1)}, f32[1024]{0:T(1024)S(1)}, f32[1024]{0:T(1024)S(1)}) all-reduce(f32[]{:T(128)} %get-tuple-element.56, ...), channel_id=1, replica_groups=mesh['dp'=16,'fsdp'=2] {'dp','fsdp'}, use_global_device_ids=true, to_apply=%region_9.10 | all-reduce | flops 10241 | bytes 81928 | tf_op jit(solution)/shard_map/psum | solution.py:235
  1152.1 14.6 fusion
  1166.6 6.4 all_to_all.88
  1173.5 6.5 all_to_all.104
  1186.5 191.9 %reduce-scatter.32.cloned.1.call-done = f32[32,6750]{1,0:T(8,128)} async-done(((f32[512,6750]{1,0:T(8,128)}), f32[32,6750]{1,0:T(8,128)}) %reduce-scatter.32.cloned.1.call-update) | async-done | bytes 864016 | tf_op jit(solution)/shard_map/reduce_scatter | solution.py:310
  1379.6 4.1 all_to_all.105
  1385.7 568.0 %reduce-scatter.20.cloned.1.call-done = f32[64,6750]{1,0:T(8,128)} async-done(((f32[1024,6750]{1,0:T(8,128)}), f32[64,6750]{1,0:T(8,128)}) %reduce-scatter.20.cloned.1.call-update) | async-done | bytes 1728016 | tf_op jit(solution)/shard_map/reduce_scatter | solution.py:309
  1955.3 4.7 all_to_all.106
  1963.9 106.1 %reduce-scatter.24.cloned.1.call-done = f32[32,1024]{1,0:T(8,128)} async-done(((f32[1024,1024]{1,0:T(8,128)}), f32[32,1024]{1,0:T(8,128)}) %reduce-scatter.24.cloned.1.call-update) | async-done | bytes 131088 | tf_op jit(solution)/shard_map/reduce_scatter | solution.py:291
  2070.1 140.0 %reduce-scatter.30.cloned.1.call-done = f32[32,1024]{1,0:T(8,128)} async-done(((f32[1024,1024]{1,0:T(8,128)}), f32[32,1024]{1,0:T(8,128)}) %reduce-scatter.30.cloned.1.call-update) | async-done | bytes 131088 | tf_op jit(solution)/shard_map/reduce_scatter | solution.py:300
  2210.1 191.0 %reduce-scatter.22.cloned.1.call-done = f32[32,3072]{1,0:T(8,128)} async-done(((f32[1024,3072]{1,0:T(8,128)}), f32[32,3072]{1,0:T(8,128)}) %reduce-scatter.22.cloned.1.call-update) | async-done | bytes 393232 | tf_op jit(solution)/shard_map/reduce_scatter | solution.py:290
  2401.1 187.2 %reduce-scatter.26.cloned.1.call-done = f32[32,4096]{1,0:T(8,128)} async-done(((f32[1024,4096]{1,0:T(8,128)}), f32[32,4096]{1,0:T(8,128)}) %reduce-scatter.26.cloned.1.call-update) | async-done | bytes 524304 | tf_op jit(solution)/shard_map/reduce_scatter | solution.py:292
  2588.4 187.4 %reduce-scatter.28.cloned.1.call-done = f32[128,1024]{1,0:T(8,128)} async-done(((f32[4096,1024]{1,0:T(8,128)}), f32[128,1024]{1,0:T(8,128)}) %reduce-scatter.28.cloned.1.call-update) | async-done | bytes 524304 | tf_op jit(solution)/shard_map/reduce_scatter | solution.py:294
  (333 shorter events, 99.5 us)
Async XLA Ops:
  16.0 52.0 %collective-permute-start = (bf16[64,6750]{1,0:T(8,128)(2,1)}, bf16[64,6750]{1,0:T(8,128)(2,1)}, u32[]{:S(2)}, u32[]{:S(2)}) collective-permute-start(bf16[64,6750]{1,0:T(8,128)(2,1)} %bitcast.3), channel_id=1, source_target_pairs={{0,2},{2,4},{4,6},{6,8},{8,10},{10,12},{12,14},{14,16},{16,18},{18... | collective-permute-start | bytes 2592008 | tf_op jit(solution)/shard_map/ppermute | solution.py:25
  17.5 53.8 %collective-permute-start.1 = (bf16[64,6750]{1,0:T(8,128)(2,1)}, bf16[64,6750]{1,0:T(8,128)(2,1)}, u32[]{:S(2)}, u32[]{:S(2)}) collective-permute-start(bf16[64,6750]{1,0:T(8,128)(2,1)} %bitcast.3), channel_id=1, source_target_pairs={{0,30},{2,0},{4,2},{6,4},{8,6},{10,8},{12,10},{14,12},{16,14},{18,... | collective-permute-start | bytes 2592008 | tf_op jit(solution)/shard_map/ppermute | solution.py:28
  22.5 7.8 all-to-all-start.1
  26.5 484.6 %reduce-scatter.16.cloned.1.call-start = ((), (), s32[]{:S(2)}) async-start(), calls=%async_computation.17 | async-start | bytes 1572864 | tf_op jit(solution)/shard_map/reduce_scatter | solution.py:204
  59.7 259.0 %copy-start.1 = (bf16[844,8,2,128]{3,1,2,0:T(8,128)(2,1)}, bf16[844,8,2,128]{3,1,2,0:T(8,128)(2,1)S(1)}, u32[]{:S(2)}) copy-start(bf16[844,8,2,128]{3,1,2,0:T(8,128)(2,1)S(1)} %copy.137) | copy-start | bytes 10371076
  68.0 22.5 collective-permute-start.2
  71.3 38.1 %collective-permute-start.3 = (bf16[64,6750]{1,0:T(8,128)(2,1)}, bf16[64,6750]{1,0:T(8,128)(2,1)S(1)}, u32[]{:S(2)}, u32[]{:S(2)}) collective-permute-start(bf16[64,6750]{1,0:T(8,128)(2,1)} %collective-permute-done.1), channel_id=1, source_target_pairs={{0,30},{2,0},{4,2},{6,4},{8,6},{10,8},{12,10},{14,12},{16,14},{18,... | collective-permute-start | bytes 2592008 | tf_op jit(solution)/shard_map/ppermute | solution.py:28
  90.5 37.2 %collective-permute-start.4 = (bf16[64,6750]{1,0:T(8,128)(2,1)S(1)}, bf16[64,6750]{1,0:T(8,128)(2,1)S(1)}, u32[]{:S(2)}, u32[]{:S(2)}) collective-permute-start(bf16[64,6750]{1,0:T(8,128)(2,1)S(1)} %collective-permute-done.2), channel_id=1, source_target_pairs={{0,2},{2,4},{4,6},{6,8},{8,10},{10,12},{12,14},{14,16},{16,18},{18... | collective-permute-start | bytes 2592008 | tf_op jit(solution)/shard_map/ppermute | solution.py:25
  109.4 39.3 %collective-permute-start.5 = (bf16[64,6750]{1,0:T(8,128)(2,1)S(1)}, bf16[64,6750]{1,0:T(8,128)(2,1)S(1)}, u32[]{:S(2)}, u32[]{:S(2)}) collective-permute-start(bf16[64,6750]{1,0:T(8,128)(2,1)S(1)} %collective-permute-done.3), channel_id=1, source_target_pairs={{0,30},{2,0},{4,2},{6,4},{8,6},{10,8},{12,10},{14,12},{16,14},{18,... | collective-permute-start | bytes 2592008 | tf_op jit(solution)/shard_map/ppermute | solution.py:28
  127.7 38.4 %collective-permute-start.6 = (bf16[64,6750]{1,0:T(8,128)(2,1)S(1)}, bf16[64,6750]{1,0:T(8,128)(2,1)S(1)}, u32[]{:S(2)}, u32[]{:S(2)}) collective-permute-start(bf16[64,6750]{1,0:T(8,128)(2,1)S(1)} %collective-permute-done.4), channel_id=1, source_target_pairs={{0,2},{2,4},{4,6},{6,8},{8,10},{10,12},{12,14},{14,16},{16,18},{18... | collective-permute-start | bytes 2592008 | tf_op jit(solution)/shard_map/ppermute | solution.py:25
  148.7 38.5 %collective-permute-start.7 = (bf16[64,6750]{1,0:T(8,128)(2,1)S(1)}, bf16[64,6750]{1,0:T(8,128)(2,1)S(1)}, u32[]{:S(2)}, u32[]{:S(2)}) collective-permute-start(bf16[64,6750]{1,0:T(8,128)(2,1)S(1)} %collective-permute-done.5), channel_id=1, source_target_pairs={{0,30},{2,0},{4,2},{6,4},{8,6},{10,8},{12,10},{14,12},{16,14},{18,... | collective-permute-start | bytes 2592008 | tf_op jit(solution)/shard_map/ppermute | solution.py:28
  166.2 37.7 %collective-permute-start.8 = (bf16[64,6750]{1,0:T(8,128)(2,1)S(1)}, bf16[64,6750]{1,0:T(8,128)(2,1)S(1)}, u32[]{:S(2)}, u32[]{:S(2)}) collective-permute-start(bf16[64,6750]{1,0:T(8,128)(2,1)S(1)} %collective-permute-done.6), channel_id=1, source_target_pairs={{0,2},{2,4},{4,6},{6,8},{8,10},{10,12},{12,14},{14,16},{16,18},{18... | collective-permute-start | bytes 2592008 | tf_op jit(solution)/shard_map/ppermute | solution.py:25
  187.2 37.7 %collective-permute-start.9 = (bf16[64,6750]{1,0:T(8,128)(2,1)S(1)}, bf16[64,6750]{1,0:T(8,128)(2,1)S(1)}, u32[]{:S(2)}, u32[]{:S(2)}) collective-permute-start(bf16[64,6750]{1,0:T(8,128)(2,1)S(1)} %collective-permute-done.7), channel_id=1, source_target_pairs={{0,30},{2,0},{4,2},{6,4},{8,6},{10,8},{12,10},{14,12},{16,14},{18,... | collective-permute-start | bytes 2592008 | tf_op jit(solution)/shard_map/ppermute | solution.py:28
  203.9 37.8 %collective-permute-start.10 = (bf16[64,6750]{1,0:T(8,128)(2,1)S(1)}, bf16[64,6750]{1,0:T(8,128)(2,1)S(1)}, u32[]{:S(2)}, u32[]{:S(2)}) collective-permute-start(bf16[64,6750]{1,0:T(8,128)(2,1)S(1)} %collective-permute-done.8), channel_id=1, source_target_pairs={{0,2},{2,4},{4,6},{6,8},{8,10},{10,12},{12,14},{14,16},{16,18},{18... | collective-permute-start | bytes 2592008 | tf_op jit(solution)/shard_map/ppermute | solution.py:25
  224.9 37.8 %collective-permute-start.11 = (bf16[64,6750]{1,0:T(8,128)(2,1)S(1)}, bf16[64,6750]{1,0:T(8,128)(2,1)S(1)}, u32[]{:S(2)}, u32[]{:S(2)}) collective-permute-start(bf16[64,6750]{1,0:T(8,128)(2,1)S(1)} %collective-permute-done.9), channel_id=1, source_target_pairs={{0,30},{2,0},{4,2},{6,4},{8,6},{10,8},{12,10},{14,12},{16,14},{18,... | collective-permute-start | bytes 2592008 | tf_op jit(solution)/shard_map/ppermute | solution.py:28
  241.7 38.0 %collective-permute-start.12 = (bf16[64,6750]{1,0:T(8,128)(2,1)S(1)}, bf16[64,6750]{1,0:T(8,128)(2,1)S(1)}, u32[]{:S(2)}, u32[]{:S(2)}) collective-permute-start(bf16[64,6750]{1,0:T(8,128)(2,1)S(1)} %collective-permute-done.10), channel_id=1, source_target_pairs={{0,2},{2,4},{4,6},{6,8},{8,10},{10,12},{12,14},{14,16},{16,18},{18... | collective-permute-start | bytes 2592008 | tf_op jit(solution)/shard_map/ppermute | solution.py:25
  262.7 38.9 %collective-permute-start.13 = (bf16[64,6750]{1,0:T(8,128)(2,1)S(1)}, bf16[64,6750]{1,0:T(8,128)(2,1)S(1)}, u32[]{:S(2)}, u32[]{:S(2)}) collective-permute-start(bf16[64,6750]{1,0:T(8,128)(2,1)S(1)} %collective-permute-done.11), channel_id=1, source_target_pairs={{0,30},{2,0},{4,2},{6,4},{8,6},{10,8},{12,10},{14,12},{16,14},{18,... | collective-permute-start | bytes 2592008 | tf_op jit(solution)/shard_map/ppermute | solution.py:28
  279.6 38.1 %collective-permute-start.14 = (bf16[64,6750]{1,0:T(8,128)(2,1)S(1)}, bf16[64,6750]{1,0:T(8,128)(2,1)S(1)}, u32[]{:S(2)}, u32[]{:S(2)}) collective-permute-start(bf16[64,6750]{1,0:T(8,128)(2,1)S(1)} %collective-permute-done.12), channel_id=1, source_target_pairs={{0,2},{2,4},{4,6},{6,8},{8,10},{10,12},{12,14},{14,16},{16,18},{18... | collective-permute-start | bytes 2592008 | tf_op jit(solution)/shard_map/ppermute | solution.py:25
  326.9 12.4 copy-start.73
  326.9 12.6 copy-start.74
  326.9 12.8 copy-start.75
  326.9 13.1 copy-start.76
  326.9 13.3 copy-start.77
  326.9 13.5 copy-start.78
  326.9 75.7 %copy-start.69 = (bf16[128]{0:T(256)(128)(2,1)S(1)}, bf16[128]{0:T(256)(128)(2,1)}, u32[]{:S(2)}) copy-start(bf16[128]{0:T(256)(128)(2,1)} %param.34) | copy-start | bytes 772
  326.9 104.4 %copy-start.60 = (bf16[16,16]{1,0:T(8,128)(2,1)S(1)}, bf16[16,16]{1,0:T(8,128)(2,1)}, u32[]{:S(2)}) copy-start(bf16[16,16]{1,0:T(8,128)(2,1)} %param.43) | copy-start | bytes 1540
  326.9 104.5 %copy-start.61 = (bf16[16,16]{1,0:T(8,128)(2,1)S(1)}, bf16[16,16]{1,0:T(8,128)(2,1)}, u32[]{:S(2)}) copy-start(bf16[16,16]{1,0:T(8,128)(2,1)} %param.44) | copy-start | bytes 1540
  326.9 183.0 %copy-start.67 = (f32[2,128]{1,0:T(2,128)S(1)}, f32[2,128]{1,0:T(2,128)}, u32[]{:S(2)}) copy-start(f32[2,128]{1,0:T(2,128)} %param.24) | copy-start | bytes 3076
  327.0 183.0 %copy-start.65 = (s32[1,128]{1,0:T(1,128)S(1)}, s32[1,128]{1,0:T(1,128)}, u32[]{:S(2)}) copy-start(s32[1,128]{1,0:T(1,128)} %param.25) | copy-start | bytes 1540
  327.0 185.5 %all-gather.9.cloned.1.call-start = ((), (), s32[]{:S(2)}) async-start(), calls=%async_computation.18 | async-start | bytes 6488064 | tf_op jit(solution)/shard_map/all_gather | solution.py:160
  327.6 190.5 %all-gather.11.cloned.1.call-start = ((), (), s32[]{:S(2)}) async-start(), calls=%async_computation.19 | async-start | bytes 2162688 | tf_op jit(solution)/shard_map/all_gather | solution.py:161
  328.2 231.6 %all-gather.13.cloned.1.call-start = ((), (), s32[]{:S(2)}) async-start(), calls=%async_computation.20 | async-start | bytes 8650752 | tf_op jit(solution)/shard_map/all_gather | solution.py:162
  328.7 310.2 %all-gather.15.cloned.1.call-start = ((), (), s32[]{:S(2)}) async-start(), calls=%async_computation.21 | async-start | bytes 8650752 | tf_op jit(solution)/shard_map/all_gather | solution.py:164
  329.5 367.2 %all-gather.17.cloned.1.call-start = ((), (), s32[]{:S(2)}) async-start(), calls=%async_computation.22 | async-start | bytes 2162688 | tf_op jit(solution)/shard_map/all_gather | solution.py:170
  330.2 468.9 %all-gather.19.cloned.1.call-start = ((), (), s32[]{:S(2)}) async-start(), calls=%async_computation.23 | async-start | bytes 7380992 | tf_op jit(solution)/shard_map/all_gather | solution.py:202
  336.6 491.4 %reduce-scatter.18.cloned.1.call-start = ((), (), s32[]{:S(2)}) async-start(), calls=%async_computation.24 | async-start | bytes 393216 | tf_op jit(solution)/shard_map/reduce_scatter | solution.py:245
  518.0 47.9 %copy-start.18 = (bf16[16,64,128]{2,1,0:T(8,128)(2,1)}, bf16[16,64,128]{2,1,0:T(8,128)(2,1)S(1)}, u32[]{:S(2)}) copy-start(bf16[16,64,128]{2,1,0:T(8,128)(2,1)S(1)} %convolution_convert_fusion.3) | copy-start | bytes 786436
  520.7 45.2 %copy-start.40 = (f32[128]{0:T(128)}, f32[128]{0:T(128)S(1)}, u32[]{:S(2)}) copy-start(f32[128]{0:T(128)S(1)} %broadcast_multiply_fusion.1) | copy-start | bytes 1540
  520.9 45.1 %copy-start.71 = (f32[128]{0:T(128)}, f32[128]{0:T(128)S(1)}, u32[]{:S(2)}) copy-start(f32[128]{0:T(128)S(1)} %multiply_reduce_fusion.6) | copy-start | bytes 1540
  520.9 45.1 %copy-start.43 = (f32[128]{0:T(128)}, f32[128]{0:T(128)S(1)}, u32[]{:S(2)}) copy-start(f32[128]{0:T(128)S(1)} %fusion.52) | copy-start | bytes 1540
  565.9 132.9 %copy-start.55 = (s32[128]{0:T(128)S(1)}, s32[128]{0:T(128)}, u32[]{:S(2)}) copy-start(s32[128]{0:T(128)} %param.27) | copy-start | bytes 1540
  646.1 50.6 %copy-start.28 = (bf16[128,1024]{0,1:T(8,128)(2,1)}, bf16[128,1024]{0,1:T(8,128)(2,1)S(1)}, u32[]{:S(2)}) copy-start(bf16[128,1024]{0,1:T(8,128)(2,1)S(1)} %fusion.12) | copy-start | bytes 786436
  646.1 53.0 %copy-start.27 = (f32[128,512]{1,0:T(8,128)S(1)}, f32[128,512]{1,0:T(8,128)}, u32[]{:S(2)}) copy-start(f32[128,512]{1,0:T(8,128)} %param.28) | copy-start | bytes 786436
  744.9 61.6 %copy-start.62 = (f32[2,1,128]{2,1,0:T(1,128)S(1)}, f32[2,1,128]{2,1,0:T(1,128)}, u32[]{:S(2)}) copy-start(f32[2,1,128]{2,1,0:T(1,128)} %convert_element_type.194) | copy-start | bytes 3076
  812.2 112.2 %reduce-scatter.34.cloned.1.call-start = ((), (), s32[]{:S(2)}) async-start(), calls=%async_computation.32 | async-start | bytes 270336
  812.3 14.5 copy-start.58
  814.2 12.5 copy-start.34
  815.4 240.6 %reduce-scatter.36.cloned.1.call-start = ((), (), s32[]{:S(2)}) async-start(), calls=%async_computation.33 | async-start | bytes 270336
  816.6 561.7 %reduce-scatter.32.cloned.1.call-start = ((), (), s32[]{:S(2)}) async-start(), calls=%async_computation.31 | async-start | bytes 14761984 | tf_op jit(solution)/shard_map/reduce_scatter | solution.py:310
  826.8 1126.9 %reduce-scatter.20.cloned.1.call-start = ((), (), s32[]{:S(2)}) async-start(), calls=%async_computation.25 | async-start | bytes 29523968 | tf_op jit(solution)/shard_map/reduce_scatter | solution.py:309
  840.9 12.3 copy-start.72
  888.2 1181.9 %reduce-scatter.24.cloned.1.call-start = ((), (), s32[]{:S(2)}) async-start(), calls=%async_computation.27 | async-start | bytes 4325376 | tf_op jit(solution)/shard_map/reduce_scatter | solution.py:291
  891.8 1318.3 %reduce-scatter.30.cloned.1.call-start = ((), (), s32[]{:S(2)}) async-start(), calls=%async_computation.30 | async-start | bytes 4325376 | tf_op jit(solution)/shard_map/reduce_scatter | solution.py:300
  894.6 1506.5 %reduce-scatter.22.cloned.1.call-start = ((), (), s32[]{:S(2)}) async-start(), calls=%async_computation.26 | async-start | bytes 12976128 | tf_op jit(solution)/shard_map/reduce_scatter | solution.py:290
  901.1 1687.2 %reduce-scatter.26.cloned.1.call-start = ((), (), s32[]{:S(2)}) async-start(), calls=%async_computation.28 | async-start | bytes 17301504 | tf_op jit(solution)/shard_map/reduce_scatter | solution.py:292
  910.5 1865.2 %reduce-scatter.28.cloned.1.call-start = ((), (), s32[]{:S(2)}) async-start(), calls=%async_computation.29 | async-start | bytes 17301504 | tf_op jit(solution)/shard_map/reduce_scatter | solution.py:294
  920.3 137.2 %copy-start.17 = (bf16[128,512]{1,0:T(8,128)(2,1)S(1)}, bf16[128,512]{1,0:T(8,128)(2,1)}, u32[]{:S(2)}) copy-start(bf16[128,512]{1,0:T(8,128)(2,1)} %copy-done.15) | copy-start | bytes 393220
  920.3 137.2 %copy-start.46 = (f32[1024]{0:T(1024)S(1)}, f32[1024]{0:T(1024)}, u32[]{:S(2)}) copy-start(f32[1024]{0:T(1024)} %get-tuple-element.70) | copy-start | bytes 12292
  920.3 137.2 %copy-start.47 = (f32[1024]{0:T(1024)S(1)}, f32[1024]{0:T(1024)}, u32[]{:S(2)}) copy-start(f32[1024]{0:T(1024)} %get-tuple-element.76) | copy-start | bytes 12292
  920.3 137.2 %copy-start.48 = (f32[1024]{0:T(1024)S(1)}, f32[1024]{0:T(1024)}, u32[]{:S(2)}) copy-start(f32[1024]{0:T(1024)} %get-tuple-element.20) | copy-start | bytes 12292
  920.3 137.2 %copy-start.49 = (f32[1024]{0:T(1024)S(1)}, f32[1024]{0:T(1024)}, u32[]{:S(2)}) copy-start(f32[1024]{0:T(1024)} %get-tuple-element.18) | copy-start | bytes 12292
  920.3 137.2 %copy-start.50 = (f32[4096]{0:T(1024)S(1)}, f32[4096]{0:T(1024)}, u32[]{:S(2)}) copy-start(f32[4096]{0:T(1024)} %get-tuple-element.68) | copy-start | bytes 49156
  920.3 137.2 %copy-start.63 = (f32[1024]{0:T(1024)S(1)}, f32[1024]{0:T(1024)}, u32[]{:S(2)}) copy-start(f32[1024]{0:T(1024)} %get-tuple-element.74) | copy-start | bytes 12292
  920.3 231.7 %copy-start.54 = (f32[256]{0:T(256)S(1)}, f32[256]{0:T(256)}, u32[]{:S(2)}) copy-start(f32[256]{0:T(256)} %copy-done.53) | copy-start | bytes 3076
  (50 other events, 194.2 us)
Sparse Core Ops, SparseCore 0:
  327.1 31.0 reduce-scatter.15
  812.3 7.7 reduce-scatter.17
  822.3 102.0 reduce-scatter.33
  926.6 129.3 reduce-scatter.35
  1058.2 320.1 reduce-scatter.31
  1380.6 573.0 reduce-scatter.19
  1956.6 113.3 reduce-scatter.23
  2073.0 137.0 reduce-scatter.29
  2217.7 183.3 reduce-scatter.21
  2403.8 184.4 reduce-scatter.25
  2591.2 184.4 reduce-scatter.27
Sparse Core Ops, SparseCore 1:
  330.7 91.2 all-gather.8
  425.1 54.7 all-gather.10
  483.0 76.7 all-gather.12
  563.0 75.8 all-gather.14
  642.2 54.5 all-gather.16
  699.8 99.3 all-gather.18
